TPU v7x, 32 devices: a whole 2x2x4 slice. The times are simulated.
32 devices in a mesh: rec: 16 (over z, y, core), feat: 2 (over x).
Axes of the slice: x: 2, y: 2, z: 4, core: 2. Of those that a mesh axis runs over, the one named last changes fastest.
Arguments:
- real_profiles: bfloat16 [8192, 10240], P('rec', 'feat'), may hold values from -4 to 4
- synthetic_profiles: bfloat16 [1024, 10240], P('rec', 'feat'), may hold values from -10 to 10
- projection: bfloat16 [10240, 512], P('feat'), may hold values from -0.0625 to 0.0625
Outputs:
- real_min: float32 [8192], P('rec')
- synthetic_min: float32 [1024], P('rec')
All inputs are finite; a program needn't handle non-finite values.
Results may differ from a plain program's by a relative error of at most 0.0003.
Values sent between devices are 32-bit elements; how exact they have to be, the bound alone decides.
A program may use at most 64 MiB of HBM per device.

v0:
```python
import jax
import jax.numpy as jnp
from jax import lax
from jax.sharding import PartitionSpec as P


def visit_blocks(real_embed, real_norm, synth_embed, synth_norm):
    embed_width = synth_embed.shape[1]
    start_min = jnp.full((real_embed.shape[0],), jnp.inf, jnp.float32)
    best_real = start_min
    piece_embed = lax.all_gather(synth_embed, "rec", axis=0, tiled=True)
    piece_norm = lax.all_gather(synth_norm, "rec", axis=0, tiled=True)
    piece_rows = piece_embed.shape[0]
    blocks = piece_rows // 512
    embed_blocks = piece_embed.reshape(blocks, piece_rows // blocks, embed_width)
    norm_blocks = piece_norm.reshape(blocks, piece_rows // blocks)

    def one_block(best, inputs):
        block_embed, block_norm = inputs
        products = lax.dot_general(
            block_embed,
            real_embed,
            (((1,), (1,)), ((), ())),
            precision=lax.Precision.HIGHEST,
            preferred_element_type=jnp.float32,
        )
        distance = block_norm[:, None] + real_norm[None, :] - 2.0 * products
        return (jnp.minimum(best, jnp.min(distance, axis=0)), jnp.min(distance, axis=1))

    best_real, block_mins = lax.scan(one_block, best_real, (embed_blocks, norm_blocks))
    min_table = block_mins.reshape(piece_rows)
    return (best_real, min_table)


def collect(min_table, local_rows):
    combined = lax.pmin(min_table, "rec")
    return lax.dynamic_slice_in_dim(combined, lax.axis_index("rec") * local_rows, local_rows, 0)


def per_device(real_profiles, synthetic_profiles, projection):
    embed_width = projection.shape[1]
    real_part = jnp.dot(real_profiles, projection, preferred_element_type=jnp.float32)
    synth_part = jnp.dot(synthetic_profiles, projection, preferred_element_type=jnp.float32)
    real_sum, synth_sum = lax.psum((real_part, synth_part), "feat")
    real_norm = jnp.sum(jnp.square(real_sum), axis=1)
    synth_norm = jnp.sum(jnp.square(synth_sum), axis=1)
    best_real, min_table = visit_blocks(real_sum, real_norm, synth_sum, synth_norm)
    synth_best = collect(min_table, synth_sum.shape[0])
    return (best_real / embed_width, synth_best / embed_width)


def solution(mesh):
    placed = (P("rec", "feat"), P("rec", "feat"), P("feat", None))
    return jax.shard_map(
        per_device, mesh=mesh, in_specs=placed, out_specs=(P("rec"), P("rec")), check_vma=False
    )
```

profile of v0, /device:TPU:0, one launch (start us, length us, event | category | flops | bytes accessed | tf_op | source)
XLA Modules:
  0.0 153.5 jit_solution(4634444542938398693)
XLA Ops:
  7.2 0.0 copy-start
  7.2 0.0 all-reduce.4.cloned.1.call-start
  7.2 0.0 copy-start.1
  7.2 8.0 %fusion.6 = f32[512,512]{1,0:T(8,128)} fusion(bf16[512,5120]{1,0:T(8,128)(2,1)} %param.5, bf16[5120,512]{1,0:T(8,128)(2,1)} %param.7), kind=kOutput, calls=%fused_computation.13 | convolution fusion | flops 2684354560 | bytes 11534336 | tf_op jit(solution)/shard_map/dot_general | solution.py:42
  15.3 0.0 copy-done
  15.3 0.0 copy-done.1
  15.3 0.0 copy-start.2
  15.3 1.7 %fusion.5 = f32[64,512]{1,0:T(8,128)} fusion(bf16[64,5120]{1,0:T(8,128)(2,1)S(1)} %copy-done, bf16[5120,512]{1,0:T(8,128)(2,1)S(1)} %copy-done.1), kind=kOutput, calls=%fused_computation.12 | convolution fusion | flops 335544320 | bytes 6029312 | tf_op jit(solution)/shard_map/dot_general | solution.py:43
  17.0 0.0 all-reduce.4.cloned.1.call-update
  17.0 0.0 all-gather.2.cloned.1.call-start
  17.0 45.9 %all-reduce.4.cloned.1.call-done = (f32[64,512]{1,0:T(8,128)}, f32[512,512]{1,0:T(8,128)}) async-done(((f32[64,512]{1,0:T(8,128)}, f32[512,512]{1,0:T(8,128)}), (f32[64,512]{1,0:T(8,128)}, f32[512,512]{1,0:T(8,128)})) %all-reduce.4.cloned.1.call-update) | async-done | bytes 1179664 | tf_op jit(solution)/shard_map/psum | solution.py:44
  62.9 0.0 all-gather.2.cloned.1.call-update
  63.0 0.0 copy-done.2
  63.0 0.6 dynamic-slice
  64.2 1.0 multiply_reduce_fusion.1
  65.3 0.2 dynamic-update-slice
  65.5 33.5 %all-reduce = f32[1024]{0:T(1024)S(1)} all-reduce(f32[1024]{0:T(1024)S(1)} %dynamic-update-slice), channel_id=1, replica_groups=mesh['rec'=16,'feat'=2] {'rec'}, use_global_device_ids=true, to_apply=%add | all-reduce | flops 1024 | bytes 8192
  99.0 1.4 multiply_reduce_fusion
  100.4 6.4 %all-gather.2.cloned.1.call-done = f32[1024,512]{1,0:T(8,128)} async-done(((f32[64,512]{1,0:T(8,128)}), f32[1024,512]{1,0:T(8,128)}) %all-gather.2.cloned.1.call-update) | async-done | bytes 2097168 | tf_op jit(solution)/shard_map/all_gather | solution.py:11
  106.8 7.2 %while.13 = (s32[]{:T(128)}, f32[512]{0:T(512)S(1)}, f32[2,512]{1,0:T(2,128)S(1)}, f32[2,512]{1,0:T(2,128)S(1)}, f32[512]{0:T(512)S(1)}, /*index=5*/f32[2,512,51...) while((s32[]{:T(128)}, f32[512]{0:T(512)S(1)}, f32[2,512]{1,0:T(2,128)S(1)}, ...), condition=%wide.region_7.8_spmd.clone, body=%wide.region_4.7_spmd.clone.sunk | while | flops 1611923456 | bytes 2120303 | solution.py:30
  106.8 3.5 %fusion.15 = (f32[512]{0:T(512)S(1)}, f32[512]{0:T(512)S(1)}) fusion(f32[512,512]{1,0:T(8,128)} %get-tuple-element.155, f32[2,512,512]{2,1,0:T(8,128)} %get-tuple-element.154, s32[]{:T(128)} %get-tuple-element.140, f32[512]{0:T(512)S(1)} %get-tuple-element.153, f32[512]{0:T(512)S(1)} %bitcast.25), kind=kOutput, calls=%fused_computation.11.clone.1 | convolution fusion | flops 1611922432 | bytes 2105856 | tf_op jit(solution)/shard_map/while/body/eval_jaxpr/dot_general | solution.py:20
  110.4 3.5 %fusion.15 = (f32[512]{0:T(512)S(1)}, f32[512]{0:T(512)S(1)}) fusion(f32[512,512]{1,0:T(8,128)} %get-tuple-element.155, f32[2,512,512]{2,1,0:T(8,128)} %get-tuple-element.154, s32[]{:T(128)} %get-tuple-element.140, f32[512]{0:T(512)S(1)} %get-tuple-element.153, f32[512]{0:T(512)S(1)} %bitcast.25), kind=kOutput, calls=%fused_computation.11.clone.1 | convolution fusion | flops 1611922432 | bytes 2105856 | tf_op jit(solution)/shard_map/while/body/eval_jaxpr/dot_general | solution.py:20
  114.0 31.5 %pmin.7 = f32[1024]{0:T(1024)S(1)} all-reduce(f32[1024]{0:T(1024)S(1)} %bitcast.26), channel_id=1, replica_groups=mesh['rec'=16,'feat'=2] {'rec'}, use_global_device_ids=true, to_apply=%region_8.9 | all-reduce | flops 1024 | bytes 8192 | tf_op jit(solution)/shard_map/pmin | solution.py:36
  145.5 0.6 broadcast_multiply_fusion
  146.1 0.6 dynamic-slice_multiply_fusion
  (11 shorter events, 0.1 us)
Async XLA Ops:
  7.2 8.1 %copy-start = (bf16[64,5120]{1,0:T(8,128)(2,1)S(1)}, bf16[64,5120]{1,0:T(8,128)(2,1)}, u32[]{:S(2)}) copy-start(bf16[64,5120]{1,0:T(8,128)(2,1)} %param.6) | copy-start | bytes 1966084
  7.2 55.8 %all-reduce.4.cloned.1.call-start = ((), (), s32[]{:S(2)}) async-start(), calls=%async_computation.1 | async-start | bytes 2359296 | tf_op jit(solution)/shard_map/psum | solution.py:44
  7.2 8.1 %copy-start.1 = (bf16[5120,512]{1,0:T(8,128)(2,1)S(1)}, bf16[5120,512]{1,0:T(8,128)(2,1)}, u32[]{:S(2)}) copy-start(bf16[5120,512]{1,0:T(8,128)(2,1)} %param.7) | copy-start | bytes 15728644
  15.3 47.7 %copy-start.2 = (u32[32]{0:T(128)S(1)}, u32[32]{0:T(128)}, u32[]{:S(2)}) copy-start(u32[32]{0:T(128)} %constant.39) | copy-start | bytes 388
  17.0 89.8 %all-gather.2.cloned.1.call-start = ((), (), s32[]{:S(2)}) async-start(), calls=%async_computation | async-start | bytes 2228224 | tf_op jit(solution)/shard_map/all_gather | solution.py:11
Sparse Core Ops, SparseCore 0:
  17.1 45.7 all-reduce.3
  65.3 41.4 all-gather.1
where the time goes:
time: 154 us
  blocking collectives  65 us (42%)
  waiting for transfers between devices  52.3 us (34%)
  matrix products  16.8 us (11%)
  between operations  14.8 us (10%)
  other arithmetic  3.59 us (2%)
    psum x1, waiting for transfers between devices, per_device(): real_sum, synth_sum = lax.psum((real_part, synth_part), 'feat')  45.9 us
    unnamed x1, blocking collectives  33.5 us
    pmin x1, blocking collectives, collect(): combined = lax.pmin(min_table, 'rec')  31.5 us
    dot_general x1, matrix products, per_device(): jnp.dot(real_profiles, projection, preferred_element_type=jnp.float32)  8.05 us
    dot_general x2, matrix products, one_block(): lax.dot_general(block_embed, real_embed, (((1,), (1,)), ((), ())), precis...  7.08 us
    all_gather x1, waiting for transfers between devices, visit_blocks(): piece_embed = lax.all_gather(synth_embed, 'rec', axis=0, tiled=True)  6.4 us
  transfers between devices with their start and end apart: 2, of which 2 were waited for; matrix products, arithmetic and copies ran while one was open for 2% of the time, Pallas kernels for 0%

commit v1 on v0

v1 whole, which is shorter than its diff:
```python
import functools

import jax
import jax.numpy as jnp
from jax import lax
from jax.experimental import pallas as pl
from jax.experimental.pallas import tpu as pltpu
from jax.sharding import PartitionSpec as P

MESH = pl.DeviceIdType.MESH
UP_Z, DOWN_Z, UP_Y, DOWN_Y, CORE = range(5)


def split(x):
    hi = x.astype(jnp.bfloat16)
    lo = (x - hi.astype(jnp.float32)).astype(jnp.bfloat16)
    return hi, lo


def kernel(
    n_rec, n_feat, n_z, n_y, n_k,
    real_hbm, synth_hbm, proj_hbm, out_real, out_synth,
    x_v, proj_v, part, s_recv, r_recv, s_all, s_cat, s_norm, min_send, min_recv, rmin,
    in_sem, rest_sem, sx_send, sx_recv, rx_send, rx_recv, g_send, g_recv,
    m_send, m_recv, o_send, o_recv,
):
    r = lax.axis_index("rec")
    f = lax.axis_index("feat")
    c = lax.rem(r, 2)
    chip = r // 2
    y = lax.rem(chip, n_y)
    z = chip // n_y
    n_dev = n_rec * n_feat
    me = r * n_feat + f
    rows_s, genes = synth_hbm.shape
    rows_r = real_hbm.shape[0]
    width = proj_hbm.shape[1]
    own = rows_r // n_feat
    step = genes // n_k

    def chunk(q):
        start = lax.rem(f + q, n_feat) * own
        return pl.ds(pl.multiple_of(start, own), own)

    def x_rows(q):
        return pl.ds(rows_s + (q - 1) * own, own)

    loads = []
    for k in range(n_k):
        ks = pl.ds(k * step, step)
        loads.append([
            pltpu.make_async_copy(proj_hbm.at[ks], proj_v.at[ks], in_sem.at[k, 0]),
            pltpu.make_async_copy(synth_hbm.at[:, ks], x_v.at[pl.ds(0, rows_s), ks], in_sem.at[k, 1]),
            pltpu.make_async_copy(real_hbm.at[chunk(1), ks], x_v.at[x_rows(1), ks], in_sem.at[k, 2]),
        ])
        for copy in loads[-1]:
            copy.start()
    rest = []
    for q in range(2, n_feat + 1):
        rest.append(pltpu.make_async_copy(real_hbm.at[chunk(q)], x_v.at[x_rows(q)], rest_sem.at[q - 2]))
        rest[-1].start()

    barrier = pltpu.get_barrier_semaphore()

    def greet(i, carry):
        peer = lax.rem(me + i, n_dev)
        pl.semaphore_signal(
            barrier, inc=1, device_id=(peer // n_feat, lax.rem(peer, n_feat)), device_id_type=MESH
        )
        return carry

    lax.fori_loop(1, n_dev, greet, 0)

    head = rows_s + own
    for k in range(n_k):
        for copy in loads[k]:
            copy.wait()
        ks = pl.ds(k * step, step)
        term = jnp.dot(x_v[0:head, ks], proj_v[ks, :], preferred_element_type=jnp.float32)
        if k == 0:
            part[0:head, :] = term
        else:
            part[0:head, :] += term
    pl.semaphore_wait(barrier, n_dev - 1)

    s_copies, r_copies = [], []
    for q in range(1, n_feat):
        to = (r, lax.rem(f + q, n_feat))
        s_copies.append(pltpu.make_async_remote_copy(
            src_ref=part.at[pl.ds(0, rows_s)], dst_ref=s_recv.at[q - 1],
            send_sem=sx_send.at[q - 1], recv_sem=sx_recv.at[q - 1],
            device_id=to, device_id_type=MESH,
        ))
        r_copies.append(pltpu.make_async_remote_copy(
            src_ref=part.at[x_rows(q)], dst_ref=r_recv.at[q - 1],
            send_sem=rx_send.at[q - 1], recv_sem=rx_recv.at[q - 1],
            device_id=to, device_id_type=MESH,
        ))
        s_copies[-1].start()
    for q in range(2, n_feat + 1):
        rest[q - 2].wait()
        part[x_rows(q), :] = jnp.dot(x_v[x_rows(q), :], proj_v[...], preferred_element_type=jnp.float32)
    for copy in s_copies:
        copy.wait_send()
    for copy in r_copies:
        copy.start()

    def index(zz, yy, cc):
        return (zz * n_y + yy) * 2 + cc

    def forward(piece, slot):
        to = {
            UP_Z: index(z + 1, y, c), DOWN_Z: index(z - 1, y, c),
            UP_Y: index(z, y + 1, c), DOWN_Y: index(z, y - 1, c), CORE: index(z, y, 1 - c),
        }[slot]
        return pltpu.make_async_remote_copy(
            src_ref=s_all.at[piece], dst_ref=s_all.at[piece],
            send_sem=g_send.at[piece, slot], recv_sem=g_recv.at[piece],
            device_id=(to, f), device_id_type=MESH,
        )

    exists = {UP_Z: z + 1 < n_z, DOWN_Z: z > 0, UP_Y: y + 1 < n_y, DOWN_Y: y > 0}
    sends = []

    def send(piece, slot, when):
        if slot in exists:
            when = exists[slot] if when is None else jnp.logical_and(when, exists[slot])
        sends.append((piece, slot, when))
        if when is None:
            forward(piece, slot).start()
        else:
            pl.when(when)(lambda: forward(piece, slot).start())

    for copy in s_copies:
        copy.wait_recv()
    total = part[0:rows_s, :]
    for q in range(1, n_feat):
        total = total + s_recv[q - 1]
    s_all[r] = total
    for slot in (UP_Z, DOWN_Z, UP_Y, DOWN_Y, CORE):
        send(r, slot, None)

    def arrived(piece, when):
        pl.when(when)(lambda: forward(piece, CORE).wait_recv())

    for d in range(1, n_z):
        for way in (1, -1):
            zs = z - way * d
            here = zs >= 0 if way > 0 else zs < n_z
            piece = index(zs, y, c)
            arrived(piece, here)
            send(piece, UP_Z if way > 0 else DOWN_Z, here)
            for slot in (UP_Y, DOWN_Y, CORE):
                send(piece, slot, here)
    for d in range(1, n_y):
        for zd in range(n_z):
            for zway in (1, -1)[: 2 if zd else 1]:
                zs = z - zway * zd
                z_ok = zs >= 0 if zway > 0 else zs < n_z
                for way in (1, -1):
                    ys = y - way * d
                    here = jnp.logical_and(z_ok, ys >= 0 if way > 0 else ys < n_y)
                    piece = index(zs, ys, c)
                    arrived(piece, here)
                    send(piece, UP_Y if way > 0 else DOWN_Y, here)
                    send(piece, CORE, here)

    def other_core(i, carry):
        forward(2 * i + 1 - c, CORE).wait_recv()
        return carry

    lax.fori_loop(0, n_rec // 2, other_core, 0)

    pair = 2 * rows_s

    def prepare(i, carry):
        s = jnp.concatenate([s_all[2 * i], s_all[2 * i + 1]], axis=0)
        hi, lo = split(s)
        s_cat[i] = jnp.concatenate([hi, lo, hi], axis=1)
        s_norm[i] = jnp.broadcast_to(jnp.sum(s * s, axis=1, keepdims=True), (pair, 128))
        return carry

    lax.fori_loop(0, n_rec // 2, prepare, 0)

    real = part[x_rows(n_feat), :]
    for q in range(1, n_feat):
        r_copies[q - 1].wait_recv()
        real = real + r_recv[q - 1]
    hi, lo = split(real)
    r_cat = jnp.concatenate([hi, hi, lo], axis=1)
    square = jnp.sum(real * real, axis=1, keepdims=True)
    r_norm = jnp.broadcast_to(square, (own, 128)).T[0:1, :]

    def send_min(i):
        peer = lax.rem(me + i, n_dev)
        to = peer // n_feat
        return pltpu.make_async_remote_copy(
            src_ref=min_send.at[to // 2], dst_ref=min_recv.at[me],
            send_sem=m_send.at[i], recv_sem=m_recv.at[me],
            device_id=(to, lax.rem(peer, n_feat)), device_id_type=MESH,
        )

    def recv_min(i):
        peer = lax.rem(me + i, n_dev)
        return pltpu.make_async_remote_copy(
            src_ref=min_send.at[0], dst_ref=min_recv.at[peer],
            send_sem=m_send.at[i], recv_sem=m_recv.at[peer],
            device_id=(peer // n_feat, lax.rem(peer, n_feat)), device_id_type=MESH,
        )

    best = jnp.full((1, own), jnp.inf, jnp.float32)
    for i in range(n_rec // 2):
        products = lax.dot_general(
            s_cat[i], r_cat, (((1,), (1,)), ((), ())), preferred_element_type=jnp.float32
        )
        dist = (s_norm[i][:, 0:1] + r_norm) - 2.0 * products
        best = jnp.minimum(best, jnp.min(dist, axis=0, keepdims=True))
        fold = dist[:, 0:128]
        for j in range(128, own, 128):
            fold = jnp.minimum(fold, dist[:, j : j + 128])
        min_send[i] = jnp.min(fold.T, axis=0, keepdims=True)

    rmin[f] = best / width

    def start_min(i, carry):
        send_min(i).start()
        return carry

    lax.fori_loop(1, n_dev, start_min, 0)

    def send_real(q, slot):
        return pltpu.make_async_remote_copy(
            src_ref=rmin.at[slot], dst_ref=rmin.at[slot],
            send_sem=o_send.at[q - 1], recv_sem=o_recv.at[q - 1],
            device_id=(r, lax.rem(f + q, n_feat)), device_id_type=MESH,
        )

    for q in range(1, n_feat):
        send_real(q, f).start()
    min_recv[me] = min_send[r // 2]

    for q in range(1, n_feat):
        send_real(q, lax.rem(f + n_feat - q, n_feat)).wait_recv()
    for q in range(n_feat):
        out_real[:, q * own : (q + 1) * own] = rmin[q]

    def wait_min(i, carry):
        recv_min(i).wait_recv()
        return carry

    lax.fori_loop(1, n_dev, wait_min, 0)
    least = jnp.min(min_recv[...], axis=0) / width
    out_synth[...] = jnp.where(c == 0, least[:, 0:rows_s], least[:, rows_s:pair])

    for q in range(1, n_feat):
        r_copies[q - 1].wait_send()
        send_real(q, f).wait_send()
    for piece, slot, when in sends:
        if when is None:
            forward(piece, slot).wait_send()
        else:
            pl.when(when)(functools.partial(lambda p, s: forward(p, s).wait_send(), piece, slot))

    def left_min(i, carry):
        send_min(i).wait_send()
        return carry

    lax.fori_loop(1, n_dev, left_min, 0)


def per_device(n_rec, n_feat, real, synth, proj):
    rows_r, genes = real.shape
    rows_s = synth.shape[0]
    width = proj.shape[1]
    own = rows_r // n_feat
    chips = n_rec // 2
    n_z = 1 << (chips.bit_length() // 2)
    n_y = chips // n_z
    n_k = 5
    n_dev = n_rec * n_feat
    f32, bf16 = jnp.float32, jnp.bfloat16
    dma = pltpu.SemaphoreType.DMA
    real_min, synth_min = pl.pallas_call(
        functools.partial(kernel, n_rec, n_feat, n_z, n_y, n_k),
        out_shape=(jax.ShapeDtypeStruct((1, rows_r), f32), jax.ShapeDtypeStruct((1, rows_s), f32)),
        in_specs=[pl.BlockSpec(memory_space=pl.ANY)] * 3,
        out_specs=(pl.BlockSpec(memory_space=pltpu.VMEM),) * 2,
        scratch_shapes=[
            pltpu.VMEM((rows_s + rows_r, genes), bf16),
            pltpu.VMEM((genes, width), bf16),
            pltpu.VMEM((rows_s + rows_r, width), f32),
            pltpu.VMEM((n_feat - 1, rows_s, width), f32),
            pltpu.VMEM((n_feat - 1, own, width), f32),
            pltpu.VMEM((n_rec, rows_s, width), f32),
            pltpu.VMEM((n_rec // 2, 2 * rows_s, 3 * width), bf16),
            pltpu.VMEM((n_rec // 2, 2 * rows_s, 128), f32),
            pltpu.VMEM((n_rec // 2, 1, 2 * rows_s), f32),
            pltpu.VMEM((n_dev, 1, 2 * rows_s), f32),
            pltpu.VMEM((n_feat, 1, own), f32),
            dma((n_k, 3)), dma((n_feat - 1,)),
            dma((n_feat - 1,)), dma((n_feat - 1,)), dma((n_feat - 1,)), dma((n_feat - 1,)),
            dma((n_rec, 5)), dma((n_rec,)),
            dma((n_dev,)), dma((n_dev,)), dma((n_feat - 1,)), dma((n_feat - 1,)),
        ],
        compiler_params=pltpu.CompilerParams(
            collective_id=0, has_side_effects=True, vmem_limit_bytes=56 * 1024 * 1024
        ),
        cost_estimate=pl.CostEstimate(
            flops=2 * (rows_r + rows_s) * genes * width + 6 * own * n_rec * rows_s * width,
            bytes_accessed=2 * genes * (rows_r + rows_s + width), transcendentals=0,
        ),
    )(real, synth, proj)
    return real_min.reshape(rows_r), synth_min.reshape(rows_s)


def solution(mesh):
    placed = (P("rec", "feat"), P("rec", "feat"), P("feat", None))
    body = functools.partial(per_device, mesh.shape["rec"], mesh.shape["feat"])
    return jax.shard_map(
        body, mesh=mesh, in_specs=placed, out_specs=(P("rec"), P("rec")), check_vma=False
    )
```

time: 154 us -> 42.2 us (0.27)
  blocking collectives: 65 us -> 0 us
  waiting for transfers between devices: 52.3 us -> 0 us
  Pallas kernels: 0 us -> 39 us
  matrix products: 16.8 us -> 0 us
  between operations: 14.8 us -> 0.64 us
  other arithmetic: 3.59 us -> 0 us
    psum x1 -> x0, waiting for transfers between devices: 45.9 us -> none  [per_device(): real_sum, synth_sum = lax.psum((real_part, synth_part), 'feat')]
    pallas_call x0 -> x1, Pallas kernels: none -> 39 us  [per_device(): pl.pallas_call(functools.partial(kernel, n_rec, n_feat, n_z, n_y, n_k), o...]
    unnamed x1 -> x0, blocking collectives: 33.5 us -> none
    pmin x1 -> x0, blocking collectives: 31.5 us -> none  [collect(): combined = lax.pmin(min_table, 'rec')]
    dot_general x4 -> x0, matrix products: 16.8 us -> none  [the longest x1 8.05 us: per_device(): jnp.dot(real_profiles, projection, preferred_element_type=jnp.float32)]
    all_gather x1 -> x0, waiting for transfers between devices: 6.4 us -> none  [visit_blocks(): piece_embed = lax.all_gather(synth_embed, 'rec', axis=0, tiled=True)]
    reduce_sum x2 -> x0, other arithmetic: 2.4 us -> none  [the longest x1 1.38 us: per_device(): real_norm = jnp.sum(jnp.square(real_sum), axis=1)]
  transfers between devices with their start and end apart: 2 -> 0, of which waited for: 2 -> 0; matrix products, arithmetic and copies ran while one was open for 2% -> 0% of each run, Pallas kernels for 0% -> 0%
where the time goes in v1:
time: 42.2 us; the launch traced here: 42 us
  Pallas kernels  39 us (92%)
  local copies, waits for them, and re-layouts  2.39 us (6%)
  between operations  0.64 us (2%)
    pallas_call x1, Pallas kernels, per_device(): pl.pallas_call(functools.partial(kernel, n_rec, n_feat, n_z, n_y, n_k), o...  39 us
    unnamed x2, local copies, waits for them, and re-layouts  2.39 us

profile of v1, /device:TPU:0, one launch (start us, length us, event | category | flops | bytes accessed | tf_op | source)
XLA Modules:
  0.0 42.0 jit_solution(8905228682634864684)
XLA Ops:
  0.6 39.0 %shard_map.50 = (f32[1,512]{1,0:T(1,128)}, f32[1,64]{1,0:T(1,128)}) custom-call(bf16[512,5120]{1,0:T(8,128)(2,1)} %real_hbm.1, bf16[64,5120]{1,0:T(8,128)(2,1)} %synth_hbm.1, bf16[5120,512]{1,0:T(8,128)(2,1)} %proj_hbm.1), custom_call_target="tpu_custom_call" | custom-call | flops 3825205248 | bytes 11141120 | tf_op jit(solution)/shard_map/pallas_call | solution.py:283
  39.7 1.2 %copy.7 = f32[512]{0:T(512)} copy(f32[512]{0:T(512)} %bitcast.2) | data formatting | bytes 4096
  40.9 1.1 %copy.8 = f32[64]{0:T(128)} copy(f32[64]{0:T(128)} %bitcast.3) | data formatting | bytes 512

commit v2 on v1

--- a/solution.py
+++ b/solution.py
@@ -9,6 +9,7 @@
 
 MESH = pl.DeviceIdType.MESH
 UP_Z, DOWN_Z, UP_Y, DOWN_Y, CORE = range(5)
+CUTS = 2
 
 
 def split(x):
@@ -37,6 +38,7 @@
     width = proj_hbm.shape[1]
     own = rows_r // n_feat
     step = genes // n_k
+    cut = rows_s // CUTS
 
     def chunk(q):
         start = lax.rem(f + q, n_feat) * own
@@ -86,17 +88,18 @@
     s_copies, r_copies = [], []
     for q in range(1, n_feat):
         to = (r, lax.rem(f + q, n_feat))
-        s_copies.append(pltpu.make_async_remote_copy(
-            src_ref=part.at[pl.ds(0, rows_s)], dst_ref=s_recv.at[q - 1],
-            send_sem=sx_send.at[q - 1], recv_sem=sx_recv.at[q - 1],
-            device_id=to, device_id_type=MESH,
-        ))
+        for h in range(CUTS):
+            s_copies.append(pltpu.make_async_remote_copy(
+                src_ref=part.at[pl.ds(h * cut, cut)], dst_ref=s_recv.at[q - 1, h],
+                send_sem=sx_send.at[q - 1, h], recv_sem=sx_recv.at[q - 1, h],
+                device_id=to, device_id_type=MESH,
+            ))
+            s_copies[-1].start()
         r_copies.append(pltpu.make_async_remote_copy(
             src_ref=part.at[x_rows(q)], dst_ref=r_recv.at[q - 1],
             send_sem=rx_send.at[q - 1], recv_sem=rx_recv.at[q - 1],
             device_id=to, device_id_type=MESH,
         ))
-        s_copies[-1].start()
     for q in range(2, n_feat + 1):
         rest[q - 2].wait()
         part[x_rows(q), :] = jnp.dot(x_v[x_rows(q), :], proj_v[...], preferred_element_type=jnp.float32)
@@ -108,79 +111,86 @@
     def index(zz, yy, cc):
         return (zz * n_y + yy) * 2 + cc
 
-    def forward(piece, slot):
+    def forward(piece, h, slot):
         to = {
             UP_Z: index(z + 1, y, c), DOWN_Z: index(z - 1, y, c),
             UP_Y: index(z, y + 1, c), DOWN_Y: index(z, y - 1, c), CORE: index(z, y, 1 - c),
         }[slot]
         return pltpu.make_async_remote_copy(
-            src_ref=s_all.at[piece], dst_ref=s_all.at[piece],
-            send_sem=g_send.at[piece, slot], recv_sem=g_recv.at[piece],
+            src_ref=s_all.at[piece, h], dst_ref=s_all.at[piece, h],
+            send_sem=g_send.at[piece, h, slot], recv_sem=g_recv.at[piece, h],
             device_id=(to, f), device_id_type=MESH,
         )
 
     exists = {UP_Z: z + 1 < n_z, DOWN_Z: z > 0, UP_Y: y + 1 < n_y, DOWN_Y: y > 0}
+    always = z >= 0
     sends = []
 
-    def send(piece, slot, when):
-        if slot in exists:
-            when = exists[slot] if when is None else jnp.logical_and(when, exists[slot])
-        sends.append((piece, slot, when))
-        if when is None:
-            forward(piece, slot).start()
-        else:
-            pl.when(when)(lambda: forward(piece, slot).start())
-
-    for copy in s_copies:
-        copy.wait_recv()
-    total = part[0:rows_s, :]
-    for q in range(1, n_feat):
-        total = total + s_recv[q - 1]
-    s_all[r] = total
-    for slot in (UP_Z, DOWN_Z, UP_Y, DOWN_Y, CORE):
-        send(r, slot, None)
-
-    def arrived(piece, when):
-        pl.when(when)(lambda: forward(piece, CORE).wait_recv())
-
-    for d in range(1, n_z):
-        for way in (1, -1):
-            zs = z - way * d
-            here = zs >= 0 if way > 0 else zs < n_z
-            piece = index(zs, y, c)
-            arrived(piece, here)
-            send(piece, UP_Z if way > 0 else DOWN_Z, here)
-            for slot in (UP_Y, DOWN_Y, CORE):
-                send(piece, slot, here)
+    def send(piece, h, slots, when):
+        for slot in slots:
+            ok = jnp.logical_and(when, exists.get(slot, always))
+            sends.append((piece, h, slot, ok))
+            pl.when(ok)(functools.partial(lambda t: forward(piece, h, t).start(), slot))
+
+    def arrived(piece, h, when):
+        pl.when(when)(lambda: forward(piece, h, CORE).wait_recv())
+
+    for wave in range(CUTS + n_z - 1):
+        if wave < CUTS:
+            total = part[wave * cut : (wave + 1) * cut, :]
+            for q in range(1, n_feat):
+                s_copies[(q - 1) * CUTS + wave].wait_recv()
+                total = total + s_recv[q - 1, wave]
+            s_all[r, wave] = total
+            send(r, wave, (UP_Z, DOWN_Z, UP_Y, DOWN_Y, CORE), always)
+        for d in range(1, n_z):
+            h = wave - d
+            if not 0 <= h < CUTS:
+                continue
+            for way in (1, -1):
+                zs = z - way * d
+                here = zs >= 0 if way > 0 else zs < n_z
+                piece = index(zs, y, c)
+                arrived(piece, h, here)
+                send(piece, h, (UP_Z if way > 0 else DOWN_Z, UP_Y, DOWN_Y, CORE), here)
+
+    pair = 2 * rows_s
+
+    def prepare(i, when):
+        def body():
+            for h in range(CUTS):
+                forward(2 * i + 1 - c, h, CORE).wait_recv()
+            rows = jnp.concatenate(
+                [s_all[2 * i].reshape(rows_s, width), s_all[2 * i + 1].reshape(rows_s, width)], axis=0
+            )
+            hi, lo = split(rows)
+            s_cat[i] = jnp.concatenate([hi, lo, hi], axis=1)
+            s_norm[i] = jnp.broadcast_to(jnp.sum(rows * rows, axis=1, keepdims=True), (pair, 128))
+
+        pl.when(when)(body)
+
+    todo = []
+    order = [(zd, way) for zd in range(n_z) for way in (1, -1)[: 2 if zd else 1]]
+    for zd, zway in order:
+        zs = z - zway * zd
+        z_ok = zs >= 0 if zway > 0 else zs < n_z
+        todo.append((zs * n_y + y, z_ok))
     for d in range(1, n_y):
-        for zd in range(n_z):
-            for zway in (1, -1)[: 2 if zd else 1]:
-                zs = z - zway * zd
-                z_ok = zs >= 0 if zway > 0 else zs < n_z
-                for way in (1, -1):
-                    ys = y - way * d
-                    here = jnp.logical_and(z_ok, ys >= 0 if way > 0 else ys < n_y)
-                    piece = index(zs, ys, c)
-                    arrived(piece, here)
-                    send(piece, UP_Y if way > 0 else DOWN_Y, here)
-                    send(piece, CORE, here)
-
-    def other_core(i, carry):
-        forward(2 * i + 1 - c, CORE).wait_recv()
-        return carry
-
-    lax.fori_loop(0, n_rec // 2, other_core, 0)
-
-    pair = 2 * rows_s
-
-    def prepare(i, carry):
-        s = jnp.concatenate([s_all[2 * i], s_all[2 * i + 1]], axis=0)
-        hi, lo = split(s)
-        s_cat[i] = jnp.concatenate([hi, lo, hi], axis=1)
-        s_norm[i] = jnp.broadcast_to(jnp.sum(s * s, axis=1, keepdims=True), (pair, 128))
-        return carry
-
-    lax.fori_loop(0, n_rec // 2, prepare, 0)
+        for zd, zway in order:
+            zs = z - zway * zd
+            z_ok = zs >= 0 if zway > 0 else zs < n_z
+            for way in (1, -1):
+                ys = y - way * d
+                here = jnp.logical_and(z_ok, ys >= 0 if way > 0 else ys < n_y)
+                piece = index(zs, ys, c)
+                for h in range(CUTS):
+                    arrived(piece, h, here)
+                    send(piece, h, (UP_Y if way > 0 else DOWN_Y, CORE), here)
+                todo.append((zs * n_y + ys, here))
+            if len(todo) > 2:
+                prepare(*todo.pop(0))
+    for item in todo:
+        prepare(*item)
 
     real = part[x_rows(n_feat), :]
     for q in range(1, n_feat):
@@ -191,42 +201,40 @@
     square = jnp.sum(real * real, axis=1, keepdims=True)
     r_norm = jnp.broadcast_to(square, (own, 128)).T[0:1, :]
 
-    def send_min(i):
-        peer = lax.rem(me + i, n_dev)
+    def send_min(peer):
         to = peer // n_feat
         return pltpu.make_async_remote_copy(
             src_ref=min_send.at[to // 2], dst_ref=min_recv.at[me],
-            send_sem=m_send.at[i], recv_sem=m_recv.at[me],
+            send_sem=m_send.at[peer], recv_sem=m_recv.at[me],
             device_id=(to, lax.rem(peer, n_feat)), device_id_type=MESH,
         )
 
-    def recv_min(i):
-        peer = lax.rem(me + i, n_dev)
+    def recv_min(peer):
         return pltpu.make_async_remote_copy(
             src_ref=min_send.at[0], dst_ref=min_recv.at[peer],
-            send_sem=m_send.at[i], recv_sem=m_recv.at[peer],
+            send_sem=m_send.at[peer], recv_sem=m_recv.at[peer],
             device_id=(peer // n_feat, lax.rem(peer, n_feat)), device_id_type=MESH,
         )
 
     best = jnp.full((1, own), jnp.inf, jnp.float32)
-    for i in range(n_rec // 2):
+    for b in range(n_rec // 4):
         products = lax.dot_general(
-            s_cat[i], r_cat, (((1,), (1,)), ((), ())), preferred_element_type=jnp.float32
-        )
-        dist = (s_norm[i][:, 0:1] + r_norm) - 2.0 * products
+            s_cat[2 * b : 2 * b + 2].reshape(2 * pair, 3 * width), r_cat,
+            (((1,), (1,)), ((), ())), preferred_element_type=jnp.float32,
+        )
+        norm = s_norm[2 * b : 2 * b + 2].reshape(2 * pair, 128)[:, 0:1]
+        dist = (norm + r_norm) - 2.0 * products
         best = jnp.minimum(best, jnp.min(dist, axis=0, keepdims=True))
         fold = dist[:, 0:128]
         for j in range(128, own, 128):
             fold = jnp.minimum(fold, dist[:, j : j + 128])
-        min_send[i] = jnp.min(fold.T, axis=0, keepdims=True)
+        least = jnp.min(fold.T, axis=0, keepdims=True)
+        min_send[2 * b] = least[:, 0:pair]
+        min_send[2 * b + 1] = least[:, pair : 2 * pair]
+        for peer in range(4 * b * n_feat, 4 * (b + 1) * n_feat):
+            pl.when(peer != me)(functools.partial(lambda p: send_min(p).start(), peer))
 
     rmin[f] = best / width
-
-    def start_min(i, carry):
-        send_min(i).start()
-        return carry
-
-    lax.fori_loop(1, n_dev, start_min, 0)
 
     def send_real(q, slot):
         return pltpu.make_async_remote_copy(
@@ -245,7 +253,7 @@
         out_real[:, q * own : (q + 1) * own] = rmin[q]
 
     def wait_min(i, carry):
-        recv_min(i).wait_recv()
+        recv_min(lax.rem(me + i, n_dev)).wait_recv()
         return carry
 
     lax.fori_loop(1, n_dev, wait_min, 0)
@@ -255,17 +263,19 @@
     for q in range(1, n_feat):
         r_copies[q - 1].wait_send()
         send_real(q, f).wait_send()
-    for piece, slot, when in sends:
-        if when is None:
-            forward(piece, slot).wait_send()
-        else:
-            pl.when(when)(functools.partial(lambda p, s: forward(p, s).wait_send(), piece, slot))
+    for piece, h, slot, when in sends:
+        pl.when(when)(functools.partial(lambda *t: forward(*t).wait_send(), piece, h, slot))
 
     def left_min(i, carry):
-        send_min(i).wait_send()
+        send_min(lax.rem(me + i, n_dev)).wait_send()
         return carry
 
     lax.fori_loop(1, n_dev, left_min, 0)
+
+
+def finish(real_ref, synth_ref, out_real, out_synth):
+    out_real[...] = real_ref[...]
+    out_synth[...] = synth_ref[...]
 
 
 def per_device(n_rec, n_feat, real, synth, proj):
@@ -289,17 +299,17 @@
             pltpu.VMEM((rows_s + rows_r, genes), bf16),
             pltpu.VMEM((genes, width), bf16),
             pltpu.VMEM((rows_s + rows_r, width), f32),
-            pltpu.VMEM((n_feat - 1, rows_s, width), f32),
+            pltpu.VMEM((n_feat - 1, CUTS, rows_s // CUTS, width), f32),
             pltpu.VMEM((n_feat - 1, own, width), f32),
-            pltpu.VMEM((n_rec, rows_s, width), f32),
+            pltpu.VMEM((n_rec, CUTS, rows_s // CUTS, width), f32),
             pltpu.VMEM((n_rec // 2, 2 * rows_s, 3 * width), bf16),
             pltpu.VMEM((n_rec // 2, 2 * rows_s, 128), f32),
             pltpu.VMEM((n_rec // 2, 1, 2 * rows_s), f32),
             pltpu.VMEM((n_dev, 1, 2 * rows_s), f32),
             pltpu.VMEM((n_feat, 1, own), f32),
             dma((n_k, 3)), dma((n_feat - 1,)),
-            dma((n_feat - 1,)), dma((n_feat - 1,)), dma((n_feat - 1,)), dma((n_feat - 1,)),
-            dma((n_rec, 5)), dma((n_rec,)),
+            dma((n_feat - 1, CUTS)), dma((n_feat - 1, CUTS)), dma((n_feat - 1,)), dma((n_feat - 1,)),
+            dma((n_rec, CUTS, 5)), dma((n_rec, CUTS)),
             dma((n_dev,)), dma((n_dev,)), dma((n_feat - 1,)), dma((n_feat - 1,)),
         ],
         compiler_params=pltpu.CompilerParams(
@@ -310,6 +320,12 @@
             bytes_accessed=2 * genes * (rows_r + rows_s + width), transcendentals=0,
         ),
     )(real, synth, proj)
+    real_min, synth_min = pl.pallas_call(
+        finish,
+        out_shape=(jax.ShapeDtypeStruct((1, rows_r), f32), jax.ShapeDtypeStruct((1, rows_s), f32)),
+        in_specs=[pl.BlockSpec(memory_space=pltpu.VMEM)] * 2,
+        out_specs=(pl.BlockSpec(memory_space=pltpu.VMEM),) * 2,
+    )(real_min, synth_min)
     return real_min.reshape(rows_r), synth_min.reshape(rows_s)
 
 

time: 42.2 us -> 37.3 us (0.88)
  Pallas kernels: 39 us -> 36.5 us
  local copies, waits for them, and re-layouts: 2.39 us -> 0 us
    pallas_call x1, Pallas kernels: 39 us -> 35.2 us  [per_device(): pl.pallas_call(functools.partial(kernel, n_rec, n_feat, n_z, n_y, n_k), o...]
    unnamed x2 -> x0, local copies, waits for them, and re-layouts: 2.39 us -> none
    pallas_call x0 -> x1, Pallas kernels: none -> 1.26 us  [per_device(): pl.pallas_call(finish, out_shape=(jax.ShapeDtypeStruct((1, rows_r), f32),...]
where the time goes in v2:
time: 37.3 us; the launch traced here: 37.1 us
  Pallas kernels  36.5 us (98%)
  between operations  0.64 us (2%)
    pallas_call x1, Pallas kernels, per_device(): pl.pallas_call(functools.partial(kernel, n_rec, n_feat, n_z, n_y, n_k), o...  35.2 us
    pallas_call x1, Pallas kernels, per_device(): pl.pallas_call(finish, out_shape=(jax.ShapeDtypeStruct((1, rows_r), f32),...  1.26 us

profile of v2, /device:TPU:0, one launch (start us, length us, event | category | flops | bytes accessed | tf_op | source)
XLA Modules:
  0.0 37.1 jit_solution(15518940762697489781)
XLA Ops:
  0.6 35.2 %shard_map.50 = (f32[1,512]{1,0:T(1,128)}, f32[1,64]{1,0:T(1,128)}) custom-call(bf16[512,5120]{1,0:T(8,128)(2,1)} %real_hbm.1, bf16[64,5120]{1,0:T(8,128)(2,1)} %synth_hbm.1, bf16[5120,512]{1,0:T(8,128)(2,1)} %proj_hbm.1), custom_call_target="tpu_custom_call" | custom-call | flops 3825205248 | bytes 11141120 | tf_op jit(solution)/shard_map/pallas_call | solution.py:293
  35.9 1.3 %shard_map.51 = (f32[1,512]{1,0:T(1,128)}, f32[1,64]{1,0:T(1,128)}) custom-call(f32[1,512]{1,0:T(1,128)} %get-tuple-element.6.real_ref, f32[1,64]{1,0:T(1,128)} %get-tuple-element.7.synth_ref), custom_call_target="tpu_custom_call" | custom-call | tf_op jit(solution)/shard_map/pallas_call | solution.py:323

commit v3 on v2

--- a/solution.py
+++ b/solution.py
@@ -248,19 +248,6 @@
     min_recv[me] = min_send[r // 2]
 
     for q in range(1, n_feat):
-        send_real(q, lax.rem(f + n_feat - q, n_feat)).wait_recv()
-    for q in range(n_feat):
-        out_real[:, q * own : (q + 1) * own] = rmin[q]
-
-    def wait_min(i, carry):
-        recv_min(lax.rem(me + i, n_dev)).wait_recv()
-        return carry
-
-    lax.fori_loop(1, n_dev, wait_min, 0)
-    least = jnp.min(min_recv[...], axis=0) / width
-    out_synth[...] = jnp.where(c == 0, least[:, 0:rows_s], least[:, rows_s:pair])
-
-    for q in range(1, n_feat):
         r_copies[q - 1].wait_send()
         send_real(q, f).wait_send()
     for piece, h, slot, when in sends:
@@ -271,6 +258,19 @@
         return carry
 
     lax.fori_loop(1, n_dev, left_min, 0)
+
+    for q in range(1, n_feat):
+        send_real(q, lax.rem(f + n_feat - q, n_feat)).wait_recv()
+    for q in range(n_feat):
+        out_real[:, q * own : (q + 1) * own] = rmin[q]
+
+    def wait_min(i, carry):
+        recv_min(lax.rem(me + i, n_dev)).wait_recv()
+        return carry
+
+    lax.fori_loop(1, n_dev, wait_min, 0)
+    least = jnp.min(min_recv[...], axis=0) / width
+    out_synth[...] = jnp.where(c == 0, least[:, 0:rows_s], least[:, rows_s:pair])
 
 
 def finish(real_ref, synth_ref, out_real, out_synth):

time: 37.3 us -> 36.7 us (0.984)
  Pallas kernels: 36.5 us -> 35.8 us
    pallas_call x1, Pallas kernels: 35.2 us -> 34.6 us  [per_device(): pl.pallas_call(functools.partial(kernel, n_rec, n_feat, n_z, n_y, n_k), o...]
where the time goes in v3:
time: 36.7 us; the launch traced here: 36.5 us
  Pallas kernels  35.8 us (98%)
  between operations  0.64 us (2%)
    pallas_call x1, Pallas kernels, per_device(): pl.pallas_call(functools.partial(kernel, n_rec, n_feat, n_z, n_y, n_k), o...  34.6 us
    pallas_call x1, Pallas kernels, per_device(): pl.pallas_call(finish, out_shape=(jax.ShapeDtypeStruct((1, rows_r), f32),...  1.26 us

profile of v3, /device:TPU:0, one launch (start us, length us, event | category | flops | bytes accessed | tf_op | source)
XLA Modules:
  0.0 36.5 jit_solution(5989708967158522640)
XLA Ops:
  0.6 34.6 %shard_map.50 = (f32[1,512]{1,0:T(1,128)}, f32[1,64]{1,0:T(1,128)}) custom-call(bf16[512,5120]{1,0:T(8,128)(2,1)} %real_hbm.1, bf16[64,5120]{1,0:T(8,128)(2,1)} %synth_hbm.1, bf16[5120,512]{1,0:T(8,128)(2,1)} %proj_hbm.1), custom_call_target="tpu_custom_call" | custom-call | flops 3825205248 | bytes 11141120 | tf_op jit(solution)/shard_map/pallas_call | solution.py:293
  35.2 1.3 %shard_map.51 = (f32[1,512]{1,0:T(1,128)}, f32[1,64]{1,0:T(1,128)}) custom-call(f32[1,512]{1,0:T(1,128)} %get-tuple-element.6.real_ref, f32[1,64]{1,0:T(1,128)} %get-tuple-element.7.synth_ref), custom_call_target="tpu_custom_call" | custom-call | tf_op jit(solution)/shard_map/pallas_call | solution.py:323

commit v4 on v3

--- a/solution.py
+++ b/solution.py
@@ -189,9 +189,6 @@
                 todo.append((zs * n_y + ys, here))
             if len(todo) > 2:
                 prepare(*todo.pop(0))
-    for item in todo:
-        prepare(*item)
-
     real = part[x_rows(n_feat), :]
     for q in range(1, n_feat):
         r_copies[q - 1].wait_recv()
@@ -200,6 +197,9 @@
     r_cat = jnp.concatenate([hi, hi, lo], axis=1)
     square = jnp.sum(real * real, axis=1, keepdims=True)
     r_norm = jnp.broadcast_to(square, (own, 128)).T[0:1, :]
+
+    for item in todo:
+        prepare(*item)
 
     def send_min(peer):
         to = peer // n_feat

time: 36.7 us -> 36.8 us (level)
  no operation moved by 1% of the time
where the time goes in v4:
time: 36.8 us; the launch traced here: 36.7 us
  Pallas kernels  36 us (98%)
  between operations  0.64 us (2%)
    pallas_call x1, Pallas kernels, per_device(): pl.pallas_call(functools.partial(kernel, n_rec, n_feat, n_z, n_y, n_k), o...  34.8 us
    pallas_call x1, Pallas kernels, per_device(): pl.pallas_call(finish, out_shape=(jax.ShapeDtypeStruct((1, rows_r), f32),...  1.26 us

profile of v4, /device:TPU:0, one launch (start us, length us, event | category | flops | bytes accessed | tf_op | source)
XLA Modules:
  0.0 36.7 jit_solution(5057854154904736807)
XLA Ops:
  0.6 34.8 %shard_map.50 = (f32[1,512]{1,0:T(1,128)}, f32[1,64]{1,0:T(1,128)}) custom-call(bf16[512,5120]{1,0:T(8,128)(2,1)} %real_hbm.1, bf16[64,5120]{1,0:T(8,128)(2,1)} %synth_hbm.1, bf16[5120,512]{1,0:T(8,128)(2,1)} %proj_hbm.1), custom_call_target="tpu_custom_call" | custom-call | flops 3825205248 | bytes 11141120 | tf_op jit(solution)/shard_map/pallas_call | solution.py:293
  35.4 1.3 %shard_map.51 = (f32[1,512]{1,0:T(1,128)}, f32[1,64]{1,0:T(1,128)}) custom-call(f32[1,512]{1,0:T(1,128)} %get-tuple-element.6.real_ref, f32[1,64]{1,0:T(1,128)} %get-tuple-element.7.synth_ref), custom_call_target="tpu_custom_call" | custom-call | tf_op jit(solution)/shard_map/pallas_call | solution.py:323
